TPU v7x, 128 devices: a whole 4x4x4 slice. The times are simulated.
128 devices in a mesh: dp: 32 (over y, z, core), expert: 4 (over x).
Axes of the slice: x: 4, y: 4, z: 4, core: 2. Of those that a mesh axis runs over, the one named last changes fastest.
Arguments:
- tokens: bfloat16 [768, 4096], P(('dp', 'expert')), may hold values from -6 to 6
- cotangent: bfloat16 [768, 4096], P(('dp', 'expert')), may hold values from -2 to 2
- route_ids: int32 [768, 2], P(('dp', 'expert')), may hold values from 0 to 3, all different within a row; in each aligned block of 6 rows (0 to 5, 6 to 11, ...) at most 4 rows name the same one
- gate_values: bfloat16 [768, 2], P(('dp', 'expert')), may hold values from 0.19921875 to 1
- gate_weight: bfloat16 [4, 4096, 14336], P('expert', None, 'dp'), may hold values from -0.09375 to 0.09375
- up_weight: bfloat16 [4, 4096, 14336], P('expert', None, 'dp'), may hold values from -0.09375 to 0.09375
- down_weight: bfloat16 [4, 14336, 4096], P('expert', 'dp'), may hold values from -0.046875 to 0.046875
- gate_direction: bfloat16 [4, 4096, 14336], P('expert', None, 'dp'), may hold values from -0.09375 to 0.09375
- up_direction: bfloat16 [4, 4096, 14336], P('expert', None, 'dp'), may hold values from -0.09375 to 0.09375
Outputs:
- gate_curvature: bfloat16 [4, 4096, 14336], P('expert', None, 'dp')
- up_curvature: bfloat16 [4, 4096, 14336], P('expert', None, 'dp')
Inputs may be any that keep to these rules, and one draw needn't show every extreme that they name: `route_ids`: the two ids of a row differ. In the rows of one device (aligned blocks of 6 rows) no expert is named more than 4 times, a bound that some block reaches.
All inputs are finite; a program needn't handle non-finite values.
Results may differ from a plain program's by a relative error of at most 0.0057.
Values may be sent and summed in bfloat16 or wider, within the bound.
A program may use at most 128 MiB of HBM per device.

v0:
```python
import jax
import jax.numpy as jnp
from jax import lax
from jax.sharding import PartitionSpec as P

TOP = 2


def slopes(pre):
    sig = jax.nn.sigmoid(pre)
    first = sig * (1.0 + pre * (1.0 - sig))
    second = sig * (1.0 - sig) * (2.0 + pre * (1.0 - 2.0 * sig))
    return (first, second)


def curvature(rows_x, rows_g, w_gate, w_up, w_down, d_gate, d_up):
    gate_pre = jnp.dot(rows_x, w_gate, preferred_element_type=jnp.float32)
    up_pre = jnp.dot(rows_x, w_up, preferred_element_type=jnp.float32)
    gate_tan = jnp.dot(rows_x, d_gate, preferred_element_type=jnp.float32)
    up_tan = jnp.dot(rows_x, d_up, preferred_element_type=jnp.float32)
    hidden_grad = lax.dot_general(
        rows_g, w_down, (((1,), (1,)), ((), ())), preferred_element_type=jnp.float32
    )
    first, second = slopes(gate_pre)
    gate_term = (hidden_grad * (second * gate_tan * up_pre + first * up_tan)).astype(jnp.bfloat16)
    up_term = (hidden_grad * first * gate_tan).astype(jnp.bfloat16)
    gate_sum = lax.dot_general(
        rows_x, gate_term, (((0,), (0,)), ((), ())), preferred_element_type=jnp.float32
    )
    up_sum = lax.dot_general(
        rows_x, up_term, (((0,), (0,)), ((), ())), preferred_element_type=jnp.float32
    )
    return (gate_sum, up_sum)


def local(
    tokens,
    cotangent,
    route_ids,
    gate_values,
    gate_weight,
    up_weight,
    down_weight,
    gate_direction,
    up_direction,
):
    owner_count = lax.axis_size("expert")
    local_experts = gate_weight.shape[0]
    experts_all = local_experts * owner_count
    token_count = tokens.shape[0]
    width = tokens.shape[1]
    capacity = token_count * TOP * 4 // (3 * experts_all)
    expert_ids = jnp.arange(experts_all, dtype=jnp.int32)
    matches = route_ids[:, :, None] == expert_ids[None, None, :]
    token_weight = jnp.sum(
        jnp.where(matches, gate_values.astype(jnp.float32)[:, :, None], jnp.float32(0.0)), axis=1
    )
    routed = jnp.any(matches, axis=1).astype(jnp.int32)
    position = jnp.cumsum(routed, axis=0) - routed
    slot_ids = jnp.arange(capacity, dtype=jnp.int32)
    dispatch = (routed.T[:, None, :] == 1) & (position.T[:, None, :] == slot_ids[None, :, None])
    dispatch = dispatch.astype(jnp.bfloat16)
    scaled = (token_weight[:, :, None] * cotangent.astype(jnp.float32)[:, None, :]).astype(
        jnp.bfloat16
    )
    slot_rows = jnp.einsum(
        "ect,td->ecd", dispatch, tokens, preferred_element_type=jnp.float32
    ).astype(jnp.bfloat16)
    slot_grads = jnp.einsum(
        "ect,ted->ecd", dispatch, scaled, preferred_element_type=jnp.float32
    ).astype(jnp.bfloat16)
    slot_rows = slot_rows.reshape(owner_count, local_experts, capacity, width)
    slot_grads = slot_grads.reshape(owner_count, local_experts, capacity, width)
    grouped_rows, grouped_grads = (
        lax.all_gather(slot_rows[None], "dp", axis=0, tiled=True),
        lax.all_gather(slot_grads[None], "dp", axis=0, tiled=True),
    )
    arrived_rows, arrived_grads = (
        lax.all_to_all(grouped_rows, "expert", split_axis=1, concat_axis=1, tiled=True),
        lax.all_to_all(grouped_grads, "expert", split_axis=1, concat_axis=1, tiled=True),
    )
    flat_x = arrived_rows[:, :, 0].reshape(-1, width)
    flat_g = arrived_grads[:, :, 0].reshape(-1, width)
    gate_sum, up_sum = curvature(
        flat_x,
        flat_g,
        gate_weight[0],
        up_weight[0],
        down_weight[0],
        gate_direction[0],
        up_direction[0],
    )
    gate_parts = [gate_sum]
    up_parts = [up_sum]
    gate_acc = jnp.stack(gate_parts)
    up_acc = jnp.stack(up_parts)
    return (gate_acc.astype(jnp.bfloat16), up_acc.astype(jnp.bfloat16))


def solution(mesh):
    placed = (
        P(("dp", "expert"), None),
        P(("dp", "expert"), None),
        P(("dp", "expert"), None),
        P(("dp", "expert"), None),
        P("expert", None, "dp"),
        P("expert", None, "dp"),
        P("expert", "dp", None),
        P("expert", None, "dp"),
        P("expert", None, "dp"),
    )
    return jax.shard_map(
        local,
        mesh=mesh,
        in_specs=placed,
        out_specs=(P("expert", None, "dp"), P("expert", None, "dp")),
        check_vma=False,
    )
```

profile of v0, /device:TPU:1, one launch (start us, length us, event | category | flops | bytes accessed | tf_op | source)
XLA Modules:
  0.0 225.1 jit_solution(17539872476046673240)
XLA Ops:
  7.2 0.7 fusion.41
  8.1 0.8 convolution_convert_fusion.3
  9.7 0.8 convert_element_type.43
  10.5 0.7 select_reduce_fusion
  11.2 0.9 convolution_convert_fusion.2
  12.2 48.7 %all-gather.5.cloned.1.call-done = bf16[128,4,4096]{2,1,0:T(4,128)(2,1)} async-done(((bf16[4,4,4096]{2,1,0:T(4,128)(2,1)}), bf16[128,4,4096]{2,1,0:T(4,128)(2,1)}) %all-gather.5.cloned.1.call-update) | async-done | bytes 4194320 | tf_op jit(solution)/shard_map/all_gather | solution.py:75
  60.9 7.8 %copy.23 = bf16[32,4,1,4,4096]{4,3,0,2,1:T(4,128)(2,1)} copy(bf16[32,4,1,4,4096]{4,3,1,0,2:T(4,128)(2,1)} %bitcast.51) | data formatting | bytes 8388608 | tf_op jit(solution)/shard_map/all_gather | solution.py:75
  68.8 4.8 %all-to-all-start = ((bf16[32,4,1,4,4096]{4,3,0,2,1:T(4,128)(2,1)}), bf16[32,4,1,4,4096]{4,3,0,2,1:T(4,128)(2,1)}, u32[]{:S(2)}, u32[]{:S(2)}) async-start(bf16[32,4,1,4,4096]{4,3,0,2,1:T(4,128)(2,1)} %copy.23), calls=%async_computation | async-start | bytes 8388608 | tf_op jit(solution)/shard_map/all_to_all | solution.py:79
  73.6 35.9 %all-gather.7.cloned.1.call-done = bf16[128,4,4096]{2,1,0:T(4,128)(2,1)} async-done(((bf16[4,4,4096]{2,1,0:T(4,128)(2,1)}), bf16[128,4,4096]{2,1,0:T(4,128)(2,1)}) %all-gather.7.cloned.1.call-update) | async-done | bytes 4194320 | tf_op jit(solution)/shard_map/all_gather | solution.py:76
  109.5 7.9 %copy.25 = bf16[32,4,1,4,4096]{4,3,0,2,1:T(4,128)(2,1)} copy(bf16[32,4,1,4,4096]{4,3,1,0,2:T(4,128)(2,1)} %bitcast.52) | data formatting | bytes 8388608 | tf_op jit(solution)/shard_map/all_gather | solution.py:76
  117.4 5.0 %all-to-all-done = bf16[32,4,1,4,4096]{4,3,0,2,1:T(4,128)(2,1)} async-done(((bf16[32,4,1,4,4096]{4,3,0,2,1:T(4,128)(2,1)}), bf16[32,4,1,4,4096]{4,3,0,2,1:T(4,128)(2,1)}, u32[]{:S(2)}, u32[]{:S(2)}) %all-to-all-start) | async-done | bytes 4194336 | tf_op jit(solution)/shard_map/all_to_all | solution.py:79
  122.3 4.9 %all-to-all-start.1 = ((bf16[32,4,1,4,4096]{4,3,0,2,1:T(4,128)(2,1)}), bf16[32,4,1,4,4096]{4,3,0,2,1:T(4,128)(2,1)}, u32[]{:S(2)}, u32[]{:S(2)}) async-start(bf16[32,4,1,4,4096]{4,3,0,2,1:T(4,128)(2,1)} %copy.25), calls=%async_computation.1 | async-start | bytes 8388608 | tf_op jit(solution)/shard_map/all_to_all | solution.py:80
  127.3 7.8 %copy.24 = bf16[32,4,1,4,4096]{4,3,1,0,2:T(4,128)(2,1)} copy(bf16[32,4,1,4,4096]{4,3,0,2,1:T(4,128)(2,1)} %all-to-all-done) | data formatting | bytes 8388608 | tf_op jit(solution)/shard_map/all_to_all | solution.py:79
  135.1 6.9 %reshape_squeeze.6 = bf16[512,4096]{1,0:T(8,128)(2,1)} reshape(bf16[32,4,1,4,4096]{4,3,1,0,2:T(4,128)(2,1)} %copy.24) | data formatting | bytes 8388608 | tf_op jit(solution)/shard_map/reshape;squeeze | solution.py:82
  142.0 33.1 %all-to-all-done.1 = bf16[32,4,1,4,4096]{4,3,0,2,1:T(4,128)(2,1)} async-done(((bf16[32,4,1,4,4096]{4,3,0,2,1:T(4,128)(2,1)}), bf16[32,4,1,4,4096]{4,3,0,2,1:T(4,128)(2,1)}, u32[]{:S(2)}, u32[]{:S(2)}) %all-to-all-start.1) | async-done | bytes 4194336 | tf_op jit(solution)/shard_map/all_to_all | solution.py:80
  175.1 7.9 %copy.26 = bf16[32,4,1,4,4096]{4,3,1,0,2:T(4,128)(2,1)} copy(bf16[32,4,1,4,4096]{4,3,0,2,1:T(4,128)(2,1)} %all-to-all-done.1) | data formatting | bytes 8388608 | tf_op jit(solution)/shard_map/all_to_all | solution.py:80
  183.0 6.9 %reshape_squeeze.7 = bf16[512,4096]{1,0:T(8,128)(2,1)} reshape(bf16[32,4,1,4,4096]{4,3,1,0,2:T(4,128)(2,1)} %copy.26) | data formatting | bytes 8388608 | tf_op jit(solution)/shard_map/reshape;squeeze | solution.py:83
  189.9 5.5 %fusion.8 = f32[512,448]{0,1:T(8,128)S(1)} fusion(bf16[512,4096]{1,0:T(8,128)(2,1)} %reshape_squeeze.6, bf16[1,4096,448]{1,2,0:T(8,128)(2,1)} %param.13), kind=kOutput, calls=%fused_computation.12 | convolution fusion | flops 1879048192 | bytes 8781824 | tf_op jit(solution)/shard_map/dot_general | solution.py:17
  195.5 2.1 fusion.6
  197.7 1.1 copy-done.5
  198.8 2.3 %fusion.10 = f32[512,448]{0,1:T(8,128)S(1)} fusion(bf16[512,4096]{1,0:T(8,128)(2,1)S(1)} %copy-done.3, bf16[1,448,4096]{2,1,0:T(8,128)(2,1)S(1)} %copy-done.5), kind=kOutput, calls=%fused_computation.14 | convolution fusion | flops 1879048192 | bytes 8781824 | tf_op jit(solution)/shard_map/dot_general | solution.py:21
  201.1 2.4 %fusion.12 = f32[512,448]{0,1:T(8,128)S(1)} fusion(bf16[512,4096]{1,0:T(8,128)(2,1)S(1)} %copy-done.2, bf16[1,4096,448]{1,2,0:T(8,128)(2,1)S(1)} %copy-done.6, f32[512,448]{0,1:T(8,128)S(1)} %fusion.6, f32[512,448]{0,1:T(8,128)S(1)} %fusion.8), kind=kOutput, calls=%fused_computation.16 | convolution fusion | flops 1881800704 | bytes 10616832 | tf_op jit(solution)/shard_map/dot_general | solution.py:18
  203.5 4.2 %fusion.1 = bf16[1,4096,448]{1,2,0:T(8,128)(2,1)} fusion(bf16[512,4096]{1,0:T(8,128)(2,1)S(1)} %copy-done.2, f32[512,448]{0,1:T(8,128)S(1)} %fusion.6, f32[512,448]{0,1:T(8,128)S(1)} %fusion.10, f32[512,448]{0,1:T(8,128)S(1)} %fusion.8), kind=kOutput, calls=%fused_computation.3 | convolution fusion | flops 1883176960 | bytes 10616832 | tf_op jit(solution)/shard_map/dot_general | solution.py:30
  207.7 10.6 %fusion = bf16[1,4096,448]{1,2,0:T(8,128)(2,1)} fusion(bf16[512,4096]{1,0:T(8,128)(2,1)} %reshape_squeeze.6, f32[512,448]{0,1:T(8,128)S(1)} %fusion.10, f32[512,448]{0,1:T(8,128)S(1)} %fusion.12, bf16[1,4096,448]{1,2,0:T(8,128)(2,1)} %param.17, f32[512,448]{0,1:T(8,128)S(1)} %fusion.8), kind=kOutput, calls=%fused_computation.2 | convolution fusion | flops 3762454528 | bytes 14286848 | tf_op jit(solution)/shard_map/dot_general | solution.py:27
  (21 shorter events, 1.2 us)
Async XLA Ops:
  7.2 1.0 copy-start
  7.2 53.8 %all-gather.5.cloned.1.call-start = ((), (), s32[]{:S(2)}) async-start(), calls=%async_computation.2 | async-start | bytes 4325376 | tf_op jit(solution)/shard_map/all_gather | solution.py:75
  9.0 100.5 %all-gather.7.cloned.1.call-start = ((), (), s32[]{:S(2)}) async-start(), calls=%async_computation.3 | async-start | bytes 4325376 | tf_op jit(solution)/shard_map/all_gather | solution.py:76
  68.8 53.6 %all-to-all-start = ((bf16[32,4,1,4,4096]{4,3,0,2,1:T(4,128)(2,1)}), bf16[32,4,1,4,4096]{4,3,0,2,1:T(4,128)(2,1)}, u32[]{:S(2)}, u32[]{:S(2)}) async-start(bf16[32,4,1,4,4096]{4,3,0,2,1:T(4,128)(2,1)} %copy.23), calls=%async_computation | async-start | bytes 8388608 | tf_op jit(solution)/shard_map/all_to_all | solution.py:79
  122.3 52.8 %all-to-all-start.1 = ((bf16[32,4,1,4,4096]{4,3,0,2,1:T(4,128)(2,1)}), bf16[32,4,1,4,4096]{4,3,0,2,1:T(4,128)(2,1)}, u32[]{:S(2)}, u32[]{:S(2)}) async-start(bf16[32,4,1,4,4096]{4,3,0,2,1:T(4,128)(2,1)} %copy.25), calls=%async_computation.1 | async-start | bytes 8388608 | tf_op jit(solution)/shard_map/all_to_all | solution.py:80
  189.9 5.5 %copy-start.2 = (bf16[512,4096]{1,0:T(8,128)(2,1)S(1)}, bf16[512,4096]{1,0:T(8,128)(2,1)}, u32[]{:S(2)}) copy-start(bf16[512,4096]{1,0:T(8,128)(2,1)} %reshape_squeeze.6) | copy-start | bytes 12582916
  189.9 5.6 %copy-start.4 = (bf16[1,4096,448]{1,2,0:T(8,128)(2,1)S(1)}, bf16[1,4096,448]{1,2,0:T(8,128)(2,1)}, u32[]{:S(2)}) copy-start(bf16[1,4096,448]{1,2,0:T(8,128)(2,1)} %param.16) | copy-start | bytes 11010052
  195.5 2.2 copy-start.3
  195.5 3.3 %copy-start.5 = (bf16[1,448,4096]{2,1,0:T(8,128)(2,1)S(1)}, bf16[1,448,4096]{2,1,0:T(8,128)(2,1)}, u32[]{:S(2)}) copy-start(bf16[1,448,4096]{2,1,0:T(8,128)(2,1)} %param.15) | copy-start | bytes 11010052
  198.8 2.3 %copy-start.6 = (bf16[1,4096,448]{1,2,0:T(8,128)(2,1)S(1)}, bf16[1,4096,448]{1,2,0:T(8,128)(2,1)}, u32[]{:S(2)}) copy-start(bf16[1,4096,448]{1,2,0:T(8,128)(2,1)} %param.14) | copy-start | bytes 11010052
  207.7 10.6 %copy-start.1 = (bf16[6,4096]{1,0:T(8,128)(2,1)S(1)}, bf16[6,4096]{1,0:T(8,128)(2,1)}, u32[]{:S(2)}) copy-start(bf16[6,4096]{1,0:T(8,128)(2,1)} %param.9) | copy-start | bytes 147460
Sparse Core Ops, SparseCore 0:
  10.8 50.0 all-gather.4
  63.8 45.6 all-gather.6
where the time goes:
time: 227 us; the launch traced here: 225 us
  waiting for transfers between devices  123 us (54%)
  local copies, waits for them, and re-layouts  46.5 us (20%)
  matrix products  28.8 us (13%)
  between operations  14.1 us (6%)
  starting transfers between devices  9.83 us (4%)
  other arithmetic  3.1 us (1%)
    all_gather x1, waiting for transfers between devices, local(): lax.all_gather(slot_rows[None], 'dp', axis=0, tiled=True)  48.7 us
    all_gather x1, waiting for transfers between devices, local(): lax.all_gather(slot_grads[None], 'dp', axis=0, tiled=True)  35.9 us
    all_to_all x1, waiting for transfers between devices, local(): lax.all_to_all(grouped_grads, 'expert', split_axis=1, concat_axis=1, tile...  33.1 us
    dot_general x1, matrix products, curvature(): lax.dot_general(rows_x, gate_term, (((0,), (0,)), ((), ())), preferred_el...  10.6 us
    all_to_all x1, local copies, waits for them, and re-layouts, local(): lax.all_to_all(grouped_grads, 'expert', split_axis=1, concat_axis=1, tile...  7.88 us
    all_gather x1, local copies, waits for them, and re-layouts, local(): lax.all_gather(slot_grads[None], 'dp', axis=0, tiled=True)  7.88 us
    all_to_all x1, local copies, waits for them, and re-layouts, local(): lax.all_to_all(grouped_rows, 'expert', split_axis=1, concat_axis=1, tiled...  7.83 us
    all_gather x1, local copies, waits for them, and re-layouts, local(): lax.all_gather(slot_rows[None], 'dp', axis=0, tiled=True)  7.83 us
  transfers between devices with their start and end apart: 4, of which 4 were waited for; matrix products, arithmetic and copies ran while one was open for 15% of the time, Pallas kernels for 0%

commit v1 on v0

v1 whole, which is shorter than its diff:
```python
import functools

import jax
import jax.numpy as jnp
from jax import lax
from jax.experimental import pallas as pl
from jax.experimental.pallas import tpu as pltpu
from jax.sharding import PartitionSpec as P

MESH = pl.DeviceIdType.MESH
NT = (((1,), (1,)), ((), ()))
TN = (((0,), (0,)), ((), ()))
META = 128
CHUNKS = 8
VMEM_LIMIT = 56 * 2**20


def dispatch_matrix(ids, gates, ring):
    row = lax.broadcasted_iota(jnp.int32, (16, 128), 0)
    lane = lax.broadcasted_iota(jnp.int32, (16, 128), 1)
    expert = lane >> 5
    kind = (lane >> 4) & 1
    here = (((lane >> 2) & 3) == ring) & ((row >> 3) == kind)
    slot = lane & 3
    taken = jnp.zeros((16, 128), jnp.int32)
    out = jnp.zeros((16, 128), jnp.float32)
    for t in range(ids.shape[1]):
        first = jnp.broadcast_to(ids[0:1, t : t + 1], (16, 128)) == expert
        second = jnp.broadcast_to(ids[1:2, t : t + 1], (16, 128)) == expert
        gate = jnp.where(
            first,
            jnp.broadcast_to(gates[0:1, t : t + 1], (16, 128)),
            jnp.broadcast_to(gates[1:2, t : t + 1], (16, 128)),
        )
        routed = first | second
        value = jnp.where(kind == 0, jnp.float32(1.0), gate)
        hit = routed & here & (taken == slot) & ((row & 7) == t)
        out = jnp.where(hit, value, out)
        taken = taken + routed.astype(jnp.int32)
    return out.astype(jnp.bfloat16)


def front(
    tok,
    cot,
    ids,
    gates,
    wg,
    wu,
    dg,
    du,
    wd,
    xout,
    terms,
    raw,
    outbox,
    rows,
    weights,
    acc,
    raw_send,
    raw_recv,
    x_send,
    x_recv,
    ring_send,
    ring_recv,
    half_send,
    half_recv,
    sib_send,
    sib_recv,
    w_sem,
    xout_sem,
):
    n = CHUNKS
    width = tok.shape[1] // n
    hidden = wg.shape[0]
    dp = lax.axis_index("dp")
    x = lax.axis_index("expert")
    y, z, core = dp // 8, (dp // 2) % 4, dp % 2
    q = jnp.where(core == 0, y, z)
    r = jnp.where(core == 0, z, y)

    def plane(q_at, r_at, c_at):
        q_at, r_at = lax.rem(q_at, 4), lax.rem(r_at, 4)
        y_at = jnp.where(core == 0, q_at, r_at)
        z_at = jnp.where(core == 0, r_at, q_at)
        return (y_at * 4 + z_at) * 2 + c_at

    raw_to = [(plane(q + d, r, core), x) for d in (1, 3, 2)]
    x_to = [(dp, lax.rem(x + d, 4)) for d in (1, 3, 2)]
    ring_to = [(plane(q, r + d, core), x) for d in (1, 3)]
    sibling = (dp + 1 - 2 * core, x)

    barrier = pltpu.get_barrier_semaphore()
    partners = raw_to + x_to + ring_to + [sibling]
    for device in partners:
        pl.semaphore_signal(barrier, inc=1, device_id=device, device_id_type=MESH)

    def weight_copies(k):
        return [
            pltpu.make_async_copy(
                w.at[:, pl.ds(pl.multiple_of(k * width, width), width)],
                weights.at[k, j],
                w_sem.at[k],
            )
            for j, w in enumerate((wg, wu, dg, du, wd))
        ]

    raw[q] = jnp.zeros(raw.shape[1:], raw.dtype)
    raw[q, 0:6, META:] = tok[...]
    raw[q, 8:14, META:] = cot[...]
    raw[q, :, 0:META] = dispatch_matrix(ids[...], gates[...].astype(jnp.float32), q)

    pl.semaphore_wait(barrier, len(partners))

    def raw_columns(k):
        if k == 0:
            return pl.ds(0, META + width)
        return pl.ds(META + k * width, width)

    def raw_copy(k, i, source):
        return pltpu.make_async_remote_copy(
            src_ref=raw.at[q, :, raw_columns(k)],
            dst_ref=raw.at[source, :, raw_columns(k)],
            send_sem=raw_send.at[i],
            recv_sem=raw_recv.at[k, i],
            device_id=raw_to[i],
            device_id_type=MESH,
        )

    for k in range(n):
        for i in range(3):
            raw_copy(k, i, q).start()

    @pl.loop(0, n)
    def _(k):
        for copy in weight_copies(k):
            copy.start()

    acc[...] = jnp.zeros_like(acc)

    def x_copy(k, i):
        to = lax.rem(x + (1, 3, 2)[i], 4)
        return pltpu.make_async_remote_copy(
            src_ref=outbox.at[k, to],
            dst_ref=rows.at[k, :, core, r, x],
            send_sem=x_send.at[i],
            recv_sem=x_recv.at[k, i],
            device_id=x_to[i],
            device_id_type=MESH,
        )

    def select(k):
        columns = pl.ds(pl.multiple_of(META + k * width, 128), width)
        blocks = raw[:, :, columns].reshape(64, width)
        matrix = raw[:, :, 0:META].reshape(64, META)
        slots = lax.dot_general(matrix, blocks, TN, preferred_element_type=jnp.float32)
        slots = slots.astype(jnp.bfloat16).reshape(4, 2, 16, width)
        outbox[k] = slots
        rows[k, :, core, r, x] = outbox[k, x]
        for i in range(3):
            x_copy(k, i).start()

    left, right, across = lax.rem(r + 3, 4), lax.rem(r + 1, 4), lax.rem(r + 2, 4)

    def ring_copy(k, i):
        return pltpu.make_async_remote_copy(
            src_ref=rows.at[k, :, core, r],
            dst_ref=rows.at[k, :, core, r],
            send_sem=ring_send.at[i],
            recv_sem=ring_recv.at[k, i],
            device_id=ring_to[i],
            device_id_type=MESH,
        )

    def half_copy(k, i):
        at = left if i == 0 else right
        return pltpu.make_async_remote_copy(
            src_ref=rows.at[k, i, core, at],
            dst_ref=rows.at[k, i, core, at],
            send_sem=half_send.at[i],
            recv_sem=half_recv.at[k, i],
            device_id=ring_to[i],
            device_id_type=MESH,
        )

    def sib_copy(k, i):
        at = (r, left, right, across)[i]
        return pltpu.make_async_remote_copy(
            src_ref=rows.at[k, :, core, at],
            dst_ref=rows.at[k, :, core, at],
            send_sem=sib_send.at[i],
            recv_sem=sib_recv.at[k, i],
            device_id=sibling,
            device_id_type=MESH,
        )

    def xout_copy(k):
        return pltpu.make_async_copy(rows.at[k, 0], xout.at[k], xout_sem)

    for k in range(n):
        for i in range(3):
            raw_copy(k, i, q).wait_recv()
        select(k)

    def exchange(k):
        for i in range(3):
            x_copy(k, i).wait_recv()
        for i in range(2):
            ring_copy(k, i).start()
        sib_copy(k, 0).start()

    def forward(k):
        for i in range(2):
            ring_copy(k, i).wait_recv()
        for i in range(2):
            half_copy(k, i).start()
        for i in (1, 2):
            sib_copy(k, i).start()

    def finish(k):
        for i in range(2):
            half_copy(k, i).wait_recv()
        sib_copy(k, 3).start()

    def compute(k):
        for i in range(4):
            sib_copy(k, i).wait_recv()
        xout_copy(k).start()
        pltpu.make_async_copy(weights.at[k], weights.at[k], w_sem.at[k]).wait()
        for j in range(5):
            part = rows[k, j // 4].reshape(512, width)
            acc[j] += lax.dot_general(
                weights[k, j], part, NT, preferred_element_type=jnp.float32
            )

    @pl.loop(0, n + 4)
    def _(i):
        @pl.when(i < n)
        def _():
            exchange(i)

        @pl.when((i >= 2) & (i < n + 2))
        def _():
            forward(i - 2)

        @pl.when((i >= 3) & (i < n + 3))
        def _():
            finish(i - 3)

        @pl.when(i >= 4)
        def _():
            compute(i - 4)

    @pl.loop(0, hidden // 16)
    def _(b):
        at = pl.ds(pl.multiple_of(b * 16, 16), 16)
        gate_pre, up_pre, gate_tan, up_tan = [acc[j, at, :] for j in range(4)]
        grad = acc[4, at, :]
        sig = jax.nn.sigmoid(gate_pre)
        rest = sig * (1.0 - sig)
        first = sig + gate_pre * rest
        second = rest * (2.0 + gate_pre * (1.0 - 2.0 * sig))
        terms[0, at, :] = (grad * (second * gate_tan * up_pre + first * up_tan)).astype(
            jnp.bfloat16
        )
        terms[1, at, :] = (grad * first * gate_tan).astype(jnp.bfloat16)

    for i in range(3):
        pltpu.make_async_copy(raw.at[q], raw.at[q], raw_send.at[i]).wait()
        pltpu.make_async_copy(outbox.at[:, i], outbox.at[:, i], x_send.at[i]).wait()
    for i in range(2):
        whole = rows.at[:, :, core, r]
        pltpu.make_async_copy(whole, whole, ring_send.at[i]).wait()
        half = rows.at[:, i, core, r]
        pltpu.make_async_copy(half, half, half_send.at[i]).wait()
    for i in range(4):
        whole = rows.at[:, :, core, r]
        pltpu.make_async_copy(whole, whole, sib_send.at[i]).wait()
    pltpu.make_async_copy(rows.at[:, 0], xout, xout_sem).wait()


def back(terms, x, gate, up):
    out = jnp.dot(
        terms[...].reshape(-1, terms.shape[-1]),
        x[0].reshape(terms.shape[-1], -1),
        preferred_element_type=jnp.float32,
    ).astype(jnp.bfloat16)
    hidden = terms.shape[1]
    gate[0] = out[:hidden]
    up[0] = out[hidden:]


def local(tokens, cotangent, route_ids, gate_values, w_gate, w_up, w_down, d_gate, d_up):
    width = tokens.shape[1]
    hidden = w_down.shape[1]
    n = CHUNKS
    chunk = width // n
    by_hidden = [jnp.swapaxes(w[0], 0, 1) for w in (w_gate, w_up, d_gate, d_up)]
    block = (n, 2, 4, 4, 16, chunk)
    vmem = pl.BlockSpec(memory_space=pltpu.VMEM)
    hbm = pl.BlockSpec(memory_space=pl.ANY)
    dma = pltpu.SemaphoreType.DMA
    xs, terms = pl.pallas_call(
        front,
        out_shape=(
            jax.ShapeDtypeStruct(block, jnp.bfloat16),
            jax.ShapeDtypeStruct((2, hidden, 512), jnp.bfloat16),
        ),
        in_specs=[vmem] * 4 + [hbm] * 5,
        out_specs=(hbm, vmem),
        scratch_shapes=[
            pltpu.VMEM((4, 16, META + width), jnp.bfloat16),
            pltpu.VMEM((n, 4, 2, 16, chunk), jnp.bfloat16),
            pltpu.VMEM((n, 2, 2, 4, 4, 16, chunk), jnp.bfloat16),
            pltpu.VMEM((n, 5, hidden, chunk), jnp.bfloat16),
            pltpu.VMEM((5, hidden, 512), jnp.float32),
            dma((3,)),
            dma((n, 3)),
            dma((3,)),
            dma((n, 3)),
            dma((2,)),
            dma((n, 2)),
            dma((2,)),
            dma((n, 2)),
            dma((4,)),
            dma((n, 4)),
            dma((n,)),
            dma,
        ],
        compiler_params=pltpu.CompilerParams(
            collective_id=0, has_side_effects=True, vmem_limit_bytes=VMEM_LIMIT
        ),
        name="gather_and_project",
    )(tokens, cotangent, route_ids.T, gate_values.T, *by_hidden, w_down[0])

    out = jax.ShapeDtypeStruct((1, hidden, width), jnp.bfloat16)
    gate, up = pl.pallas_call(
        back,
        grid=(n,),
        out_shape=(out, out),
        in_specs=[
            pl.BlockSpec((2, hidden, 512), lambda i: (0, 0, 0)),
            pl.BlockSpec((1, 2, 4, 4, 16, chunk), lambda i: (i, 0, 0, 0, 0, 0)),
        ],
        out_specs=[pl.BlockSpec((1, hidden, chunk), lambda i: (0, 0, i))] * 2,
        compiler_params=pltpu.CompilerParams(vmem_limit_bytes=VMEM_LIMIT),
        name="outer_products",
    )(terms, xs)
    return jnp.swapaxes(gate, 1, 2), jnp.swapaxes(up, 1, 2)


def solution(mesh):
    rows = P(("dp", "expert"), None)
    columns = P("expert", None, "dp")
    return jax.shard_map(
        local,
        mesh=mesh,
        in_specs=(rows,) * 4 + (columns, columns, P("expert", "dp", None), columns, columns),
        out_specs=(columns, columns),
        check_vma=False,
    )
```

time: 227 us -> 62.4 us (0.27)
  waiting for transfers between devices: 123 us -> 0 us
  Pallas kernels: 0 us -> 61.4 us
  local copies, waits for them, and re-layouts: 46.5 us -> 0 us
  matrix products: 28.8 us -> 0 us
  between operations: 14.1 us -> 0.64 us
  starting transfers between devices: 9.83 us -> 0 us
  other arithmetic: 3.1 us -> 0 us
    all_gather x2 -> x0, waiting for transfers between devices: 84.6 us -> none  [the longest x1 48.7 us: local(): lax.all_gather(slot_rows[None], 'dp', axis=0, tiled=True)]
    pallas_call x0 -> x2, Pallas kernels: none -> 61.4 us  [the longest x1 52.1 us: local(): pl.pallas_call(front, out_shape=(jax.ShapeDtypeStruct(block, jnp.bfloat16...]
    all_to_all x2 -> x0, waiting for transfers between devices: 38.1 us -> none  [the longest x1 33.1 us: local(): lax.all_to_all(grouped_grads, 'expert', split_axis=1, concat_axis=1, tile...]
    dot_general x8 -> x0, matrix products: 28.8 us -> none  [the longest x1 10.6 us: curvature(): lax.dot_general(rows_x, gate_term, (((0,), (0,)), ((), ())), preferred_el...]
    all_to_all x2 -> x0, local copies, waits for them, and re-layouts: 15.7 us -> none  [the longest x1 7.88 us: local(): lax.all_to_all(grouped_grads, 'expert', split_axis=1, concat_axis=1, tile...]
    all_gather x2 -> x0, local copies, waits for them, and re-layouts: 15.7 us -> none  [the longest x1 7.88 us: local(): lax.all_gather(slot_grads[None], 'dp', axis=0, tiled=True)]
    another operation x2 -> x0, local copies, waits for them, and re-layouts: 13.8 us -> none  [the longest x1 6.9 us: local(): flat_g = arrived_grads[:, :, 0].reshape(-1, width)]
    all_to_all x2 -> x0, starting transfers between devices: 9.75 us -> none  [the longest x1 4.92 us: local(): lax.all_to_all(grouped_grads, 'expert', split_axis=1, concat_axis=1, tile...]
  transfers between devices with their start and end apart: 4 -> 0, of which waited for: 4 -> 0; matrix products, arithmetic and copies ran while one was open for 15% -> 0% of each run, Pallas kernels for 0% -> 0%
where the time goes in v1:
time: 62.4 us; the launch traced here: 62 us
  Pallas kernels  61.4 us (98%)
  between operations  0.64 us (1%)
    pallas_call x1, Pallas kernels, local(): pl.pallas_call(front, out_shape=(jax.ShapeDtypeStruct(block, jnp.bfloat16...  52.1 us
    pallas_call x1, Pallas kernels, local(): pl.pallas_call(back, grid=(n,), out_shape=(out, out), in_specs=[pl.BlockS...  9.26 us

profile of v1, /device:TPU:1, one launch (start us, length us, event | category | flops | bytes accessed | tf_op | source)
XLA Modules:
  0.0 62.0 jit_solution(1003360732118845099)
XLA Ops:
  0.6 52.1 %gather_and_project.1 = (bf16[8,2,4,4,16,512]{5,4,3,2,1,0:T(8,128)(2,1)}, bf16[2,448,512]{2,1,0:T(8,128)(2,1)}) custom-call(bf16[6,4096]{1,0:T(8,128)(2,1)} %tok.1, bf16[6,4096]{1,0:T(8,128)(2,1)} %cot.1, s32[2,6]{1,0:T(2,128)} %bitcast.22, bf16[2,6]{1,0:T(2,128)(2,1)} %bitcast.23, bf16[448,4096]{1,0:T(8,128)(2,1)} %bitcast.17, bf16[448,4096]{1,0:T(8,128)(2,1)} %bitcast.18, ...), custom_call_target="tpu_custom_call" | custom-call | tf_op jit(solution)/shard_map/gather_and_project/pallas_call | solution.py:303
  52.8 9.3 %outer_products.1 = (bf16[1,448,4096]{2,1,0:T(8,128)(2,1)}, bf16[1,448,4096]{2,1,0:T(8,128)(2,1)}) custom-call(bf16[2,448,512]{2,1,0:T(8,128)(2,1)} %get-tuple-element.6.terms, bf16[8,2,4,4,16,512]{5,4,3,2,1,0:T(8,128)(2,1)} %get-tuple-element.7.x), custom_call_target="tpu_custom_call" | custom-call | tf_op jit(solution)/shard_map/outer_products/pallas_call | solution.py:337

commit v2 on v0

v2 whole, which is shorter than its diff:
```python
import jax
import jax.numpy as jnp
from jax import lax
from jax.experimental import pallas as pl
from jax.experimental.pallas import tpu as pltpu
from jax.sharding import PartitionSpec as P

MESH = pl.DeviceIdType.MESH
NT = (((1,), (1,)), ((), ()))
TN = (((0,), (0,)), ((), ()))
META = 128
CHUNKS = (512, 1024, 1024, 1024, 512)
RAW_PIECES = (1, 1, 3)
FRONT_LIMIT = 40 * 2**20
BACK_LIMIT = 20 * 2**20
STEPS = (1, 3, 2)


def stay(array):
    return pltpu.with_memory_space_constraint(array, pltpu.HBM)


def offsets(sizes):
    return [sum(sizes[:k]) for k in range(len(sizes))]


def dispatch_matrix(ids, gates, x, ring):
    row = lax.broadcasted_iota(jnp.int32, (16, 128), 0)
    lane = lax.broadcasted_iota(jnp.int32, (16, 128), 1)
    expert = ((lane >> 5) + x) & 3
    kind = (lane >> 4) & 1
    here = (((lane >> 2) & 3) == ring) & ((row >> 3) == kind)
    slot = lane & 3
    taken = jnp.zeros((16, 128), jnp.int32)
    out = jnp.zeros((16, 128), jnp.float32)
    for t in range(ids.shape[1]):
        first = jnp.broadcast_to(ids[0:1, t : t + 1], (16, 128)) == expert
        second = jnp.broadcast_to(ids[1:2, t : t + 1], (16, 128)) == expert
        gate = jnp.where(
            first,
            jnp.broadcast_to(gates[0:1, t : t + 1], (16, 128)),
            jnp.broadcast_to(gates[1:2, t : t + 1], (16, 128)),
        )
        routed = first | second
        value = jnp.where(kind == 0, jnp.float32(1.0), gate)
        hit = routed & here & (taken == slot) & ((row & 7) == t)
        out = jnp.where(hit, value, out)
        taken = taken + routed.astype(jnp.int32)
    return out.astype(jnp.bfloat16)


def front(tok, cot, ids, gates, wg, wu, dg, du, wd, *refs):
    n = len(CHUNKS)
    rows, terms = refs[:n], refs[n]
    outbox = refs[n + 1 : 2 * n + 1]
    (
        raw,
        weights,
        acc,
        raw_send,
        raw_recv,
        x_send,
        x_recv,
        ring_send,
        ring_recv,
        half_send,
        half_recv,
        sib_send,
        sib_recv,
        w_sem,
        tok_in,
        cot_in,
        ids_in,
        gates_in,
        small_sem,
    ) = refs[2 * n + 1 :]
    at = offsets(CHUNKS)
    hidden, width = weights.shape[1:]

    small_copies = [
        pltpu.make_async_copy(src, dst, small_sem.at[i])
        for i, (src, dst) in enumerate(
            ((ids, ids_in), (gates, gates_in), (tok, tok_in), (cot, cot_in))
        )
    ]
    for copy in small_copies:
        copy.start()

    dp = lax.axis_index("dp")
    x = lax.axis_index("expert")
    y, z, core = dp // 8, (dp // 2) % 4, dp % 2
    q = jnp.where(core == 0, y, z)
    r = jnp.where(core == 0, z, y)

    def plane(q_at, r_at):
        q_at, r_at = lax.rem(q_at, 4), lax.rem(r_at, 4)
        y_at = jnp.where(core == 0, q_at, r_at)
        z_at = jnp.where(core == 0, r_at, q_at)
        return (y_at * 4 + z_at) * 2 + core

    raw_to = [(plane(q + d, r), x) for d in STEPS]
    x_to = [(dp, lax.rem(x + d, 4)) for d in STEPS]
    ring_to = [(plane(q, r + d), x) for d in (1, 3)]
    sibling = (dp + 1 - 2 * core, x)

    barrier = pltpu.get_barrier_semaphore()
    partners = raw_to + x_to + ring_to + [sibling]
    for device in partners:
        pl.semaphore_signal(barrier, inc=1, device_id=device, device_id_type=MESH)

    def remote(src, dst, send, recv, device):
        return pltpu.make_async_remote_copy(
            src_ref=src,
            dst_ref=dst,
            send_sem=send,
            recv_sem=recv,
            device_id=device,
            device_id_type=MESH,
        )

    raw[0] = jnp.zeros(raw.shape[1:], raw.dtype)
    for copy in small_copies:
        copy.wait()
    raw[0, 0:6, META:] = tok_in[...]
    raw[0, 8:14, META:] = cot_in[...]
    raw[0, :, 0:META] = dispatch_matrix(ids_in[...], gates_in[...].astype(jnp.float32), x, q)

    pl.semaphore_wait(barrier, len(partners))

    ends = [META + sum(CHUNKS[: sum(RAW_PIECES[: p + 1])]) for p in range(len(RAW_PIECES))]
    raw_copies = []
    for p, end in enumerate(ends):
        columns = slice(ends[p - 1] if p else 0, end)
        raw_copies.append(
            [
                remote(
                    raw.at[0, :, columns],
                    raw.at[d, :, columns],
                    raw_send.at[i],
                    raw_recv.at[p, i],
                    raw_to[i],
                )
                for i, d in enumerate(STEPS)
            ]
        )
    for copies in raw_copies:
        for copy in copies:
            copy.start()

    weight_copies = [
        pltpu.make_async_copy(w, weights.at[j], w_sem.at[j])
        for j, w in enumerate((wg, wu, dg, du, wd))
    ]
    for copy in weight_copies:
        copy.start()

    x_copies = [
        [
            remote(
                outbox[k].at[d],
                rows[k].at[:, 0, 0, d],
                x_send.at[i],
                x_recv.at[k, i],
                x_to[i],
            )
            for i, d in enumerate(STEPS)
        ]
        for k in range(n)
    ]
    ring_copies = [
        [
            remote(
                rows[k].at[:, 0, 0],
                rows[k].at[:, 0, 1 + i],
                ring_send.at[i],
                ring_recv.at[k, i],
                ring_to[i],
            )
            for i in range(2)
        ]
        for k in range(n)
    ]
    half_copies = [
        [
            remote(
                rows[k].at[i, 0, 1 + i],
                rows[k].at[i, 0, 3],
                half_send.at[i],
                half_recv.at[k, i],
                ring_to[i],
            )
            for i in range(2)
        ]
        for k in range(n)
    ]
    sib_copies = [
        [
            remote(
                rows[k].at[:, 0, part],
                rows[k].at[:, 1, part],
                sib_send.at[i],
                sib_recv.at[k, i],
                sibling,
            )
            for i, part in enumerate((slice(0, 3), slice(3, 4)))
        ]
        for k in range(n)
    ]

    def select(k):
        if k in offsets(RAW_PIECES):
            for copy in raw_copies[offsets(RAW_PIECES).index(k)]:
                copy.wait_recv()
        size = CHUNKS[k]
        blocks = raw[:, :, META + at[k] : META + at[k] + size].reshape(64, size)
        matrix = raw[:, :, 0:META].reshape(64, META)
        slots = lax.dot_general(matrix, blocks, TN, preferred_element_type=jnp.float32)
        slots = slots.astype(jnp.bfloat16).reshape(4, 2, 16, size)
        outbox[k][...] = slots
        for copy in x_copies[k]:
            copy.start()
        rows[k][:, 0, 0, 0] = slots[0]

    def exchange(k):
        for copy in x_copies[k]:
            copy.wait_recv()
        for copy in ring_copies[k]:
            copy.start()

    def forward(k):
        for copy in ring_copies[k]:
            copy.wait_recv()
        for copy in half_copies[k]:
            copy.start()
        sib_copies[k][0].start()

    def finish(k):
        for copy in half_copies[k]:
            copy.wait_recv()
        sib_copies[k][1].start()

    def arrive(k):
        for copy in sib_copies[k]:
            copy.wait_recv()

    def product(k, j):
        size = CHUNKS[k]
        if j == 0:
            arrive(k)
        if k == 0:
            weight_copies[j].wait()
        part = rows[k][j // 4].reshape(512, size)
        value = lax.dot_general(
            weights[j, :, at[k] : at[k] + size], part, NT, preferred_element_type=jnp.float32
        )
        if k == 0:
            acc[j] = value
        else:
            acc[j] += value

    pending = []

    def fill(count):
        for _ in range(min(count, len(pending))):
            product(*pending.pop(0))

    for i in range(n + 4):
        if i < n:
            select(i)
        fill(1)
        if 0 <= i - 1 < n:
            exchange(i - 1)
        fill(1)
        if 0 <= i - 2 < n:
            forward(i - 2)
        fill(2)
        if 0 <= i - 3 < n:
            finish(i - 3)
        fill(1)
        if 0 <= i - 3 < n:
            pending.extend((i - 3, j) for j in range(5))
    fill(len(pending))

    @pl.loop(0, hidden // 16)
    def _(b):
        block = pl.ds(pl.multiple_of(b * 16, 16), 16)
        gate_pre, up_pre, gate_tan, up_tan = [acc[j, block, :] for j in range(4)]
        grad = acc[4, block, :]
        sig = jax.nn.sigmoid(gate_pre)
        rest = sig * (1.0 - sig)
        first = sig + gate_pre * rest
        second = rest * (2.0 + gate_pre * (1.0 - 2.0 * sig))
        terms[0, block, :] = (grad * (second * gate_tan * up_pre + first * up_tan)).astype(
            jnp.bfloat16
        )
        terms[1, block, :] = (grad * first * gate_tan).astype(jnp.bfloat16)

    def sent(count, sem):
        whole = weights.at[0, 0:count]
        pltpu.make_async_copy(whole, whole, sem).wait()

    for i in range(3):
        pltpu.make_async_copy(raw.at[0], raw.at[0], raw_send.at[i]).wait()
        sent(32, x_send.at[i])
    for i in range(2):
        sent(128, ring_send.at[i])
        sent(64, half_send.at[i])
    sent(384, sib_send.at[0])
    sent(128, sib_send.at[1])


def back(*refs):
    n = len(CHUNKS)
    rows, terms = refs[:n], refs[n]
    gate, up = refs[n + 1 : n + 3]
    out, out_sem = refs[n + 3 : 2 * n + 3], refs[2 * n + 3]
    at = offsets(CHUNKS)
    out_copies = []
    for k, size in enumerate(CHUNKS):
        part = rows[k][0].reshape(512, size)
        for j, to in enumerate((gate, up)):
            out[k][j] = jnp.dot(terms[j], part, preferred_element_type=jnp.float32).astype(
                jnp.bfloat16
            )
            copy = pltpu.make_async_copy(
                out[k].at[j], to.at[0, :, at[k] : at[k] + size], out_sem.at[k, j]
            )
            copy.start()
            out_copies.append(copy)
    for copy in out_copies:
        copy.wait()


def local(tokens, cotangent, route_ids, gate_values, w_gate, w_up, w_down, d_gate, d_up):
    width = tokens.shape[1]
    hidden = w_down.shape[1]
    n = len(CHUNKS)
    by_hidden = [jnp.swapaxes(w[0], 0, 1) for w in (w_gate, w_up, d_gate, d_up)]
    vmem = pl.BlockSpec(memory_space=pltpu.VMEM)
    hbm = pl.BlockSpec(memory_space=pltpu.HBM)
    dma = pltpu.SemaphoreType.DMA
    bf16 = jnp.bfloat16
    blocks = [(2, 4, 4, 16, size) for size in CHUNKS]
    held = pl.pallas_call(
        front,
        out_shape=[pltpu.VMEM((2,) + block, bf16) for block in blocks]
        + [pltpu.VMEM((2, hidden, 512), bf16)],
        in_specs=[hbm] * 9,
        out_specs=[vmem] * (n + 1),
        scratch_shapes=[pltpu.VMEM((4, 2, 16, size), bf16) for size in CHUNKS]
        + [
            pltpu.VMEM((4, 16, META + width), bf16),
            pltpu.VMEM((5, hidden, width), bf16),
            pltpu.VMEM((5, hidden, 512), jnp.float32),
            dma((3,)),
            dma((len(RAW_PIECES), 3)),
            dma((3,)),
            dma((n, 3)),
            dma((2,)),
            dma((n, 2)),
            dma((2,)),
            dma((n, 2)),
            dma((2,)),
            dma((n, 2)),
            dma((5,)),
            pltpu.VMEM(tokens.shape, bf16),
            pltpu.VMEM(cotangent.shape, bf16),
            pltpu.VMEM(route_ids.shape[::-1], jnp.int32),
            pltpu.VMEM(gate_values.shape[::-1], bf16),
            dma((4,)),
        ],
        compiler_params=pltpu.CompilerParams(
            collective_id=0, has_side_effects=True, vmem_limit_bytes=FRONT_LIMIT
        ),
        name="gather_and_project",
    )(*map(stay, (tokens, cotangent, route_ids.T, gate_values.T, *by_hidden, w_down[0])))

    out = jax.ShapeDtypeStruct((1, hidden, width), bf16)
    gate, up = pl.pallas_call(
        back,
        out_shape=(out, out),
        in_specs=[vmem] * (n + 1),
        out_specs=[hbm] * 2,
        scratch_shapes=[pltpu.VMEM((2, hidden, size), bf16) for size in CHUNKS] + [dma((n, 2))],
        compiler_params=pltpu.CompilerParams(vmem_limit_bytes=BACK_LIMIT),
        name="outer_products",
    )(*held)
    return jnp.swapaxes(gate, 1, 2), jnp.swapaxes(up, 1, 2)


def solution(mesh):
    rows = P(("dp", "expert"), None)
    columns = P("expert", None, "dp")
    return jax.shard_map(
        local,
        mesh=mesh,
        in_specs=(rows,) * 4 + (columns, columns, P("expert", "dp", None), columns, columns),
        out_specs=(columns, columns),
        check_vma=False,
    )
```

time: 227 us -> 51.5 us (0.23)
  waiting for transfers between devices: 123 us -> 0 us
  Pallas kernels: 0 us -> 50.5 us
  local copies, waits for them, and re-layouts: 46.5 us -> 0 us
  matrix products: 28.8 us -> 0 us
  between operations: 14.1 us -> 0.8 us
  starting transfers between devices: 9.83 us -> 0 us
  other arithmetic: 3.1 us -> 0 us
    all_gather x2 -> x0, waiting for transfers between devices: 84.6 us -> none  [the longest x1 48.7 us: local(): lax.all_gather(slot_rows[None], 'dp', axis=0, tiled=True)]
    pallas_call x0 -> x2, Pallas kernels: none -> 50.5 us  [the longest x1 45.7 us: local(): pl.pallas_call(front, out_shape=[pltpu.VMEM((2,) + block, bf16) for block...]
    all_to_all x2 -> x0, waiting for transfers between devices: 38.1 us -> none  [the longest x1 33.1 us: local(): lax.all_to_all(grouped_grads, 'expert', split_axis=1, concat_axis=1, tile...]
    dot_general x8 -> x0, matrix products: 28.8 us -> none  [the longest x1 10.6 us: curvature(): lax.dot_general(rows_x, gate_term, (((0,), (0,)), ((), ())), preferred_el...]
    all_to_all x2 -> x0, local copies, waits for them, and re-layouts: 15.7 us -> none  [the longest x1 7.88 us: local(): lax.all_to_all(grouped_grads, 'expert', split_axis=1, concat_axis=1, tile...]
    all_gather x2 -> x0, local copies, waits for them, and re-layouts: 15.7 us -> none  [the longest x1 7.88 us: local(): lax.all_gather(slot_grads[None], 'dp', axis=0, tiled=True)]
    another operation x2 -> x0, local copies, waits for them, and re-layouts: 13.8 us -> none  [the longest x1 6.9 us: local(): flat_g = arrived_grads[:, :, 0].reshape(-1, width)]
    all_to_all x2 -> x0, starting transfers between devices: 9.75 us -> none  [the longest x1 4.92 us: local(): lax.all_to_all(grouped_grads, 'expert', split_axis=1, concat_axis=1, tile...]
  transfers between devices with their start and end apart: 4 -> 0, of which waited for: 4 -> 0; matrix products, arithmetic and copies ran while one was open for 15% -> 0% of each run, Pallas kernels for 0% -> 0%
where the time goes in v2:
time: 51.5 us; the launch traced here: 51.3 us
  Pallas kernels  50.5 us (98%)
  between operations  0.8 us (2%)
    pallas_call x1, Pallas kernels, local(): pl.pallas_call(front, out_shape=[pltpu.VMEM((2,) + block, bf16) for block...  45.7 us
    pallas_call x1, Pallas kernels, local(): pl.pallas_call(back, out_shape=(out, out), in_specs=[vmem] * (n + 1), out...  4.85 us

profile of v2, /device:TPU:1, one launch (start us, length us, event | category | flops | bytes accessed | tf_op | source)
XLA Modules:
  0.0 51.3 jit_solution(17291257270033212229)
XLA Ops:
  0.6 45.7 %gather_and_project.1 = (bf16[2,2,4,4,16,512]{5,4,3,2,1,0:T(8,128)(2,1)S(1)}, bf16[2,2,4,4,16,1024]{5,4,3,2,1,0:T(8,128)(2,1)S(1)}, bf16[2,2,4,4,16,1024]{5,4,3,...) custom-call(bf16[6,4096]{1,0:T(8,128)(2,1)} %tok.1, ...), custom_call_target="tpu_custom_call" | custom-call | tf_op jit(solution)/shard_map/gather_and_project/pallas_call | solution.py:344
  46.3 4.8 %outer_products.1 = (bf16[1,448,4096]{2,1,0:T(8,128)(2,1)}, bf16[1,448,4096]{2,1,0:T(8,128)(2,1)}) custom-call(bf16[2,2,4,4,16,512]{5,4,3,2,1,0:T(8,128)(2,1)S(1)} %get-tuple-element.10.refs_0_, bf16[2,2,4,4,16,1024]{5,4,3,2,1,0:T(8,128)(2,1)S(1)} %get-tuple-element.11.refs_1_, bf16[2,2,4,4,16,1024]{5,4,3,2,1,0:T(8,128)(2,1)S(1)} %get-tuple-element.12.refs_2_, ...), custom_call_target="tpu_custom_call" | custom-call | tf_op jit(solution)/shard_map/outer_products/pallas_call | solution.py:379

commit v3 on v2

--- a/solution.py
+++ b/solution.py
@@ -100,7 +100,7 @@
 
     raw_to = [(plane(q + d, r), x) for d in STEPS]
     x_to = [(dp, lax.rem(x + d, 4)) for d in STEPS]
-    ring_to = [(plane(q, r + d), x) for d in (1, 3)]
+    ring_to = [(plane(q, r + d), x) for d in (1, 3, 2)]
     sibling = (dp + 1 - 2 * core, x)
 
     barrier = pltpu.get_barrier_semaphore()
@@ -176,7 +176,7 @@
                 ring_recv.at[k, i],
                 ring_to[i],
             )
-            for i in range(2)
+            for i in range(3 if k == n - 1 else 2)
         ]
         for k in range(n)
     ]
@@ -191,7 +191,7 @@
             )
             for i in range(2)
         ]
-        for k in range(n)
+        for k in range(n - 1)
     ]
     sib_copies = [
         [
@@ -204,8 +204,19 @@
             )
             for i, part in enumerate((slice(0, 3), slice(3, 4)))
         ]
-        for k in range(n)
-    ]
+        for k in range(n - 1)
+    ]
+    sib_copies.append(
+        [
+            remote(
+                rows[-1].at[:, 0],
+                rows[-1].at[:, 1],
+                sib_send.at[2],
+                sib_recv.at[n - 1, 0],
+                sibling,
+            )
+        ]
+    )
 
     def select(k):
         if k in offsets(RAW_PIECES):
@@ -230,8 +241,9 @@
     def forward(k):
         for copy in ring_copies[k]:
             copy.wait_recv()
-        for copy in half_copies[k]:
-            copy.start()
+        if k < n - 1:
+            for copy in half_copies[k]:
+                copy.start()
         sib_copies[k][0].start()
 
     def finish(k):
@@ -243,20 +255,27 @@
         for copy in sib_copies[k]:
             copy.wait_recv()
 
-    def product(k, j):
+    def product(k, owner, j):
         size = CHUNKS[k]
-        if j == 0:
+        if j == 0 and owner == 1:
             arrive(k)
-        if k == 0:
+        if k == 0 and owner == 0:
             weight_copies[j].wait()
-        part = rows[k][j // 4].reshape(512, size)
+        part = rows[k][j // 4, owner].reshape(256, size)
         value = lax.dot_general(
             weights[j, :, at[k] : at[k] + size], part, NT, preferred_element_type=jnp.float32
         )
+        lanes = slice(owner * 256, owner * 256 + 256)
         if k == 0:
-            acc[j] = value
+            acc[j, :, lanes] = value
         else:
-            acc[j] += value
+            acc[j, :, lanes] += value
+
+    def own(k):
+        pending.extend((k, 0, j) for j in range(5))
+
+    def other(k):
+        pending.extend((k, 1, j) for j in range(5))
 
     pending = []
 
@@ -264,21 +283,24 @@
         for _ in range(min(count, len(pending))):
             product(*pending.pop(0))
 
-    for i in range(n + 4):
+    for i in range(n + 3):
         if i < n:
             select(i)
-        fill(1)
+        fill(2)
         if 0 <= i - 1 < n:
             exchange(i - 1)
-        fill(1)
+        fill(2)
         if 0 <= i - 2 < n:
             forward(i - 2)
+            if i - 2 == n - 1:
+                own(n - 1)
+                other(n - 1)
+        fill(4)
+        if 0 <= i - 3 < n - 1:
+            finish(i - 3)
+            own(i - 3)
+            other(i - 3)
         fill(2)
-        if 0 <= i - 3 < n:
-            finish(i - 3)
-        fill(1)
-        if 0 <= i - 3 < n:
-            pending.extend((i - 3, j) for j in range(5))
     fill(len(pending))
 
     @pl.loop(0, hidden // 16)
@@ -295,8 +317,8 @@
         )
         terms[1, block, :] = (grad * first * gate_tan).astype(jnp.bfloat16)
 
-    def sent(count, sem):
-        whole = weights.at[0, 0:count]
+    def sent(count, sem, columns=width):
+        whole = weights.at[0, 0:count, 0:columns]
         pltpu.make_async_copy(whole, whole, sem).wait()
 
     for i in range(3):
@@ -304,9 +326,11 @@
         sent(32, x_send.at[i])
     for i in range(2):
         sent(128, ring_send.at[i])
-        sent(64, half_send.at[i])
-    sent(384, sib_send.at[0])
-    sent(128, sib_send.at[1])
+        sent(64, half_send.at[i], at[-1])
+    sent(384, sib_send.at[0], at[-1])
+    sent(128, sib_send.at[1], at[-1])
+    ring_copies[-1][2].wait_send()
+    sib_copies[-1][0].wait_send()
 
 
 def back(*refs):
@@ -356,11 +380,11 @@
             dma((len(RAW_PIECES), 3)),
             dma((3,)),
             dma((n, 3)),
+            dma((3,)),
+            dma((n, 3)),
             dma((2,)),
             dma((n, 2)),
-            dma((2,)),
-            dma((n, 2)),
-            dma((2,)),
+            dma((3,)),
             dma((n, 2)),
             dma((5,)),
             pltpu.VMEM(tokens.shape, bf16),

time: 51.5 us -> 50.9 us (0.988)
  Pallas kernels: 50.5 us -> 49.9 us
    pallas_call x1, Pallas kernels: 45.7 us -> 45.1 us  [local(): pl.pallas_call(front, out_shape=[pltpu.VMEM((2,) + block, bf16) for block...]
where the time goes in v3:
time: 50.9 us; the launch traced here: 50.7 us
  Pallas kernels  49.9 us (98%)
  between operations  0.8 us (2%)
    pallas_call x1, Pallas kernels, local(): pl.pallas_call(front, out_shape=[pltpu.VMEM((2,) + block, bf16) for block...  45.1 us
    pallas_call x1, Pallas kernels, local(): pl.pallas_call(back, out_shape=(out, out), in_specs=[vmem] * (n + 1), out...  4.85 us

profile of v3, /device:TPU:1, one launch (start us, length us, event | category | flops | bytes accessed | tf_op | source)
XLA Modules:
  0.0 50.7 jit_solution(7067082182273206386)
XLA Ops:
  0.6 45.1 %gather_and_project.1 = (bf16[2,2,4,4,16,512]{5,4,3,2,1,0:T(8,128)(2,1)S(1)}, bf16[2,2,4,4,16,1024]{5,4,3,2,1,0:T(8,128)(2,1)S(1)}, bf16[2,2,4,4,16,1024]{5,4,3,...) custom-call(bf16[6,4096]{1,0:T(8,128)(2,1)} %tok.1, ...), custom_call_target="tpu_custom_call" | custom-call | tf_op jit(solution)/shard_map/gather_and_project/pallas_call | solution.py:368
  45.7 4.8 %outer_products.1 = (bf16[1,448,4096]{2,1,0:T(8,128)(2,1)}, bf16[1,448,4096]{2,1,0:T(8,128)(2,1)}) custom-call(bf16[2,2,4,4,16,512]{5,4,3,2,1,0:T(8,128)(2,1)S(1)} %get-tuple-element.10.refs_0_, bf16[2,2,4,4,16,1024]{5,4,3,2,1,0:T(8,128)(2,1)S(1)} %get-tuple-element.11.refs_1_, bf16[2,2,4,4,16,1024]{5,4,3,2,1,0:T(8,128)(2,1)S(1)} %get-tuple-element.12.refs_2_, ...), custom_call_target="tpu_custom_call" | custom-call | tf_op jit(solution)/shard_map/outer_products/pallas_call | solution.py:403

commit v4 on v3

--- a/solution.py
+++ b/solution.py
@@ -119,11 +119,13 @@
         )
 
     raw[0] = jnp.zeros(raw.shape[1:], raw.dtype)
-    for copy in small_copies:
+    for copy in small_copies[:2]:
+        copy.wait()
+    raw[0, :, 0:META] = dispatch_matrix(ids_in[...], gates_in[...].astype(jnp.float32), x, q)
+    for copy in small_copies[2:]:
         copy.wait()
     raw[0, 0:6, META:] = tok_in[...]
     raw[0, 8:14, META:] = cot_in[...]
-    raw[0, :, 0:META] = dispatch_matrix(ids_in[...], gates_in[...].astype(jnp.float32), x, q)
 
     pl.semaphore_wait(barrier, len(partners))
 
@@ -303,7 +305,7 @@
         fill(2)
     fill(len(pending))
 
-    @pl.loop(0, hidden // 16)
+    @pl.loop(0, hidden // 16, unroll=2)
     def _(b):
         block = pl.ds(pl.multiple_of(b * 16, 16), 16)
         gate_pre, up_pre, gate_tan, up_tan = [acc[j, block, :] for j in range(4)]

time: 50.9 us -> 50.7 us (level)
  no operation moved by 1% of the time
where the time goes in v4:
time: 50.7 us; the launch traced here: 50.6 us
  Pallas kernels  49.8 us (98%)
  between operations  0.8 us (2%)
    pallas_call x1, Pallas kernels, local(): pl.pallas_call(front, out_shape=[pltpu.VMEM((2,) + block, bf16) for block...  44.9 us
    pallas_call x1, Pallas kernels, local(): pl.pallas_call(back, out_shape=(out, out), in_specs=[vmem] * (n + 1), out...  4.85 us

profile of v4, /device:TPU:1, one launch (start us, length us, event | category | flops | bytes accessed | tf_op | source)
XLA Modules:
  0.0 50.6 jit_solution(7106003449145202695)
XLA Ops:
  0.6 44.9 %gather_and_project.1 = (bf16[2,2,4,4,16,512]{5,4,3,2,1,0:T(8,128)(2,1)S(1)}, bf16[2,2,4,4,16,1024]{5,4,3,2,1,0:T(8,128)(2,1)S(1)}, bf16[2,2,4,4,16,1024]{5,4,3,...) custom-call(bf16[6,4096]{1,0:T(8,128)(2,1)} %tok.1, ...), custom_call_target="tpu_custom_call" | custom-call | tf_op jit(solution)/shard_map/gather_and_project/pallas_call | solution.py:370
  45.6 4.8 %outer_products.1 = (bf16[1,448,4096]{2,1,0:T(8,128)(2,1)}, bf16[1,448,4096]{2,1,0:T(8,128)(2,1)}) custom-call(bf16[2,2,4,4,16,512]{5,4,3,2,1,0:T(8,128)(2,1)S(1)} %get-tuple-element.10.refs_0_, bf16[2,2,4,4,16,1024]{5,4,3,2,1,0:T(8,128)(2,1)S(1)} %get-tuple-element.11.refs_1_, bf16[2,2,4,4,16,1024]{5,4,3,2,1,0:T(8,128)(2,1)S(1)} %get-tuple-element.12.refs_2_, ...), custom_call_target="tpu_custom_call" | custom-call | tf_op jit(solution)/shard_map/outer_products/pallas_call | solution.py:405
